TPU v7x, 512 devices: a whole 4x8x8 slice. The times are simulated.
512 devices in a mesh: row: 32 (over z, x), inw: 8 (over y_lo, core), outw: 2 (over y_hi).
Axes of the slice: x: 4, y: 8 (y_hi: 2, y_lo: 4; y = y_hi * 4 + y_lo), z: 8, core: 2. Of those that a mesh axis runs over, the one named last changes fastest.
Arguments:
- inputs: bfloat16 [768, 8192], P('row', ('inw', 'outw')), may hold values from -6 to 6
- out_grad: bfloat16 [768, 8192], P('row', ('inw', 'outw')), may hold values from -3 to 3
- gate_weight: bfloat16 [8192, 16384], P(('inw', 'outw'), 'row'), may hold values from -0.0625 to 0.0625
- up_weight: bfloat16 [8192, 16384], P(('inw', 'outw'), 'row'), may hold values from -0.0625 to 0.0625
- down_weight: bfloat16 [16384, 8192], P('row', ('inw', 'outw')), may hold values from -0.046875 to 0.046875
Outputs:
- grad_inputs: bfloat16 [768, 8192], P('row', ('inw', 'outw'))
- grad_gate: bfloat16 [8192, 16384], P(('inw', 'outw'), 'row')
- grad_up: bfloat16 [8192, 16384], P(('inw', 'outw'), 'row')
- grad_down: bfloat16 [16384, 8192], P('row', ('inw', 'outw'))
All inputs are finite; a program needn't handle non-finite values.
Results may differ from a plain program's by a relative error of at most 0.0049.
Values may be sent and summed in bfloat16 or wider, within the bound.
A program may use at most 64 MiB of HBM per device.

v0:
```python
import jax
import jax.numpy as jnp
from jax import lax
from jax.sharding import PartitionSpec as P


def contract_last(left, right):
    return lax.dot_general(
        left, right, (((1,), (1,)), ((), ())), preferred_element_type=jnp.float32
    )


def contract_first(left, right):
    return lax.dot_general(
        left, right, (((0,), (0,)), ((), ())), preferred_element_type=jnp.float32
    )


def swiglu_grads(gate_sum, up_sum, back_sum):
    sigmoid_gate = jax.nn.sigmoid(gate_sum)
    silu_gate = gate_sum * sigmoid_gate
    hidden = (silu_gate * up_sum).astype(jnp.bfloat16)
    gate_grad = (back_sum * up_sum * sigmoid_gate * (1.0 + gate_sum * (1.0 - sigmoid_gate))).astype(
        jnp.bfloat16
    )
    up_grad = (back_sum * silu_gate).astype(jnp.bfloat16)
    return (hidden, gate_grad, up_grad)


def per_device(inputs, out_grad, gate_weight, up_weight, down_weight):
    input_rows, grad_rows = (
        lax.all_gather(inputs, "row", axis=0, tiled=True),
        lax.all_gather(out_grad, "row", axis=0, tiled=True),
    )
    gate_part = jnp.dot(input_rows, gate_weight, preferred_element_type=jnp.float32)
    up_part = jnp.dot(input_rows, up_weight, preferred_element_type=jnp.float32)
    back_part = contract_last(grad_rows, down_weight)
    gate_sum, up_sum, back_sum = lax.psum((gate_part, up_part, back_part), ("inw", "outw"))
    hidden, gate_grad, up_grad = swiglu_grads(gate_sum, up_sum, back_sum)
    grad_down = contract_first(hidden, grad_rows).astype(jnp.bfloat16)
    grad_gate = contract_first(input_rows, gate_grad).astype(jnp.bfloat16)
    grad_up = contract_first(input_rows, up_grad).astype(jnp.bfloat16)
    grad_inputs = lax.psum_scatter(
        contract_last(gate_grad, gate_weight) + contract_last(up_grad, up_weight),
        "row",
        scatter_dimension=0,
        tiled=True,
    ).astype(jnp.bfloat16)
    return (grad_inputs, grad_gate, grad_up, grad_down)


def solution(mesh):
    in_specs = (
        P("row", ("inw", "outw")),
        P("row", ("inw", "outw")),
        P(("inw", "outw"), "row"),
        P(("inw", "outw"), "row"),
        P("row", ("inw", "outw")),
    )
    out_specs = (
        P("row", ("inw", "outw")),
        P(("inw", "outw"), "row"),
        P(("inw", "outw"), "row"),
        P("row", ("inw", "outw")),
    )
    return jax.shard_map(
        per_device, mesh=mesh, in_specs=in_specs, out_specs=out_specs, check_vma=False
    )
```

profile of v0, /device:TPU:8, one launch (start us, length us, event | category | flops | bytes accessed | tf_op | source)
XLA Modules:
  0.0 479.3 jit_solution(17125121648859528537)
XLA Ops:
  7.2 0.0 copy-start
  7.2 0.0 all-reduce.3.cloned.1.call-start
  7.2 56.1 %all_gather.7 = bf16[768,512]{1,0:T(8,128)(2,1)S(1)} all-gather(bf16[24,512]{1,0:T(8,128)(2,1)} %param.5), channel_id=1, replica_groups=mesh['row'=32,'inw'=8,'outw'=2] {'row'}, dimensions={0}, use_global_device_ids=true | all-gather | bytes 811008 | tf_op jit(solution)/shard_map/all_gather | solution.py:32
  63.3 48.7 %all_gather.6 = bf16[768,512]{1,0:T(8,128)(2,1)S(1)} all-gather(bf16[24,512]{1,0:T(8,128)(2,1)} %param.6), channel_id=1, replica_groups=mesh['row'=32,'inw'=8,'outw'=2] {'row'}, dimensions={0}, use_global_device_ids=true | all-gather | bytes 811008 | tf_op jit(solution)/shard_map/all_gather | solution.py:33
  112.0 0.0 copy-done
  112.0 1.7 fusion.7
  113.8 0.0 copy-done.2
  113.8 1.8 fusion.6
  115.6 1.7 fusion.5
  117.3 0.0 all-reduce.3.cloned.1.call-update
  117.4 0.0 reduce-scatter.2.cloned.1.call-start
  117.4 122.6 %all-reduce.3.cloned.1.call-done = (f32[768,512]{1,0:T(8,128)}, f32[768,512]{1,0:T(8,128)}, f32[768,512]{1,0:T(8,128)}) async-done(((f32[768,512]{1,0:T(8,128)}, f32[768,512]{1,0:T(8,128)}, f32[768,512]{1,0:T(8,128)}), (f32[768,512]{1,0:T(8,128)}, f32[768,512]{1,0:T(8,128)}, f32[768,512]{1,0:T(8,128)})) %all-reduce.3.cloned.1.call-update) | async-done | bytes 4718608 | tf_op jit(solution)/shard_map/psum | solution.py:38
  240.0 3.2 multiply_convert_fusion.1
  243.3 0.6 fusion.8
  243.9 0.3 copy-done.1
  244.2 1.8 convolution_add_fusion
  246.0 0.0 reduce-scatter.2.cloned.1.call-update
  246.0 0.6 fusion.1
  246.6 1.0 copy.9
  247.6 1.7 fusion.2
  249.3 1.0 copy.10
  250.3 3.3 convolution_convert_fusion
  253.7 217.4 %reduce-scatter.2.cloned.1.call-done = f32[24,512]{1,0:T(8,128)} async-done(((f32[768,512]{1,0:T(8,128)}), f32[24,512]{1,0:T(8,128)}) %reduce-scatter.2.cloned.1.call-update) | async-done | bytes 49168 | tf_op jit(solution)/shard_map/reduce_scatter | solution.py:43
  471.0 1.4 convert_element_type.29
  (4 shorter events, 0.0 us)
Async XLA Ops:
  7.2 104.9 %copy-start = (bf16[512,512]{1,0:T(8,128)(2,1)S(1)}, bf16[512,512]{1,0:T(8,128)(2,1)}, u32[]{:S(2)}) copy-start(bf16[512,512]{1,0:T(8,128)(2,1)} %param.7) | copy-start | bytes 1572868
  7.2 232.9 %all-reduce.3.cloned.1.call-start = ((), (), s32[]{:S(2)}) async-start(), calls=%async_computation.2 | async-start | bytes 9437184 | tf_op jit(solution)/shard_map/psum | solution.py:38
  112.0 1.7 copy-start.2
  113.8 1.8 copy-start.3
  117.4 353.7 %reduce-scatter.2.cloned.1.call-start = ((), (), s32[]{:S(2)}) async-start(), calls=%async_computation.1 | async-start | bytes 1622016 | tf_op jit(solution)/shard_map/reduce_scatter | solution.py:43
  243.3 0.9 copy-start.1
Sparse Core Ops, SparseCore 0:
  117.5 122.5 all-reduce.2
  246.1 224.8 reduce-scatter.1
where the time goes:
time: 480 us; the launch traced here: 479 us
  waiting for transfers between devices  340 us (71%)
  blocking collectives  105 us (22%)
  between operations  14.1 us (3%)
  matrix products  13.3 us (3%)
    reduce_scatter x1, waiting for transfers between devices, per_device(): lax.psum_scatter(contract_last(gate_grad, gate_weight) + contract_last(up...  217 us
    psum x1, waiting for transfers between devices, per_device(): lax.psum((gate_part, up_part, back_part), ('inw', 'outw'))  123 us
    all_gather x1, blocking collectives, per_device(): lax.all_gather(inputs, 'row', axis=0, tiled=True)  56.1 us
    all_gather x1, blocking collectives, per_device(): lax.all_gather(out_grad, 'row', axis=0, tiled=True)  48.7 us
  transfers between devices with their start and end apart: 2, of which 2 were waited for; matrix products, arithmetic and copies ran while one was open for 2% of the time, Pallas kernels for 0%

commit v1 on v0

--- a/solution.py
+++ b/solution.py
@@ -2,6 +2,12 @@
 import jax.numpy as jnp
 from jax import lax
 from jax.sharding import PartitionSpec as P
+
+
+def check_area(mat):
+    for k0 in ("inw", "outw"):
+        mat = lax.psum(mat, k0)
+    return mat
 
 
 def contract_last(left, right):
@@ -35,7 +41,7 @@
     gate_part = jnp.dot(input_rows, gate_weight, preferred_element_type=jnp.float32)
     up_part = jnp.dot(input_rows, up_weight, preferred_element_type=jnp.float32)
     back_part = contract_last(grad_rows, down_weight)
-    gate_sum, up_sum, back_sum = lax.psum((gate_part, up_part, back_part), ("inw", "outw"))
+    gate_sum, up_sum, back_sum = check_area((gate_part, up_part, back_part))
     hidden, gate_grad, up_grad = swiglu_grads(gate_sum, up_sum, back_sum)
     grad_down = contract_first(hidden, grad_rows).astype(jnp.bfloat16)
     grad_gate = contract_first(input_rows, gate_grad).astype(jnp.bfloat16)

time: 480 us -> 718 us (1.50)
  waiting for transfers between devices: 340 us -> 579 us
    psum x1 -> x2, waiting for transfers between devices: 123 us -> 366 us  [check_area(): mat = lax.psum(mat, k0)]
  transfers between devices with their start and end apart: 2 -> 3, of which waited for: 2 -> 3; matrix products, arithmetic and copies ran while one was open for 2% -> 1% of each run, Pallas kernels for 0% -> 0%
where the time goes in v1:
time: 718 us
  waiting for transfers between devices  579 us (81%)
  blocking collectives  105 us (15%)
  between operations  13.8 us (2%)
  matrix products  13.3 us (2%)
    psum x2, waiting for transfers between devices, check_area(): mat = lax.psum(mat, k0)  366 us
    reduce_scatter x1, waiting for transfers between devices, per_device(): lax.psum_scatter(contract_last(gate_grad, gate_weight) + contract_last(up...  213 us
    all_gather x1, blocking collectives, per_device(): lax.all_gather(inputs, 'row', axis=0, tiled=True)  56.1 us
    all_gather x1, blocking collectives, per_device(): lax.all_gather(out_grad, 'row', axis=0, tiled=True)  48.7 us
  transfers between devices with their start and end apart: 3, of which 3 were waited for; matrix products, arithmetic and copies ran while one was open for 1% of the time, Pallas kernels for 0%

profile of v1, /device:TPU:8, one launch (start us, length us, event | category | flops | bytes accessed | tf_op | source)
XLA Modules:
  0.0 718.1 jit_solution(12824255875572409208)
XLA Ops:
  7.2 0.0 all-reduce.5.cloned.1.call-start
  7.2 56.1 %all_gather.7 = bf16[768,512]{1,0:T(8,128)(2,1)S(1)} all-gather(bf16[24,512]{1,0:T(8,128)(2,1)} %param.5), channel_id=1, replica_groups=mesh['row'=32,'inw'=8,'outw'=2] {'row'}, dimensions={0}, use_global_device_ids=true | all-gather | bytes 811008 | tf_op jit(solution)/shard_map/all_gather | solution.py:38
  63.3 48.7 %all_gather.6 = bf16[768,512]{1,0:T(8,128)(2,1)S(1)} all-gather(bf16[24,512]{1,0:T(8,128)(2,1)} %param.6), channel_id=1, replica_groups=mesh['row'=32,'inw'=8,'outw'=2] {'row'}, dimensions={0}, use_global_device_ids=true | all-gather | bytes 811008 | tf_op jit(solution)/shard_map/all_gather | solution.py:39
  112.0 1.7 fusion.7
  113.8 1.8 fusion.6
  115.6 1.8 fusion.5
  117.3 0.0 all-reduce.5.cloned.1.call-update
  117.3 0.0 all-reduce.7.cloned.1.call-start
  117.4 117.4 %all-reduce.5.cloned.1.call-done = (f32[768,512]{1,0:T(8,128)}, f32[768,512]{1,0:T(8,128)}, f32[768,512]{1,0:T(8,128)}) async-done(((f32[768,512]{1,0:T(8,128)}, f32[768,512]{1,0:T(8,128)}, f32[768,512]{1,0:T(8,128)}), (f32[768,512]{1,0:T(8,128)}, f32[768,512]{1,0:T(8,128)}, f32[768,512]{1,0:T(8,128)})) %all-reduce.5.cloned.1.call-update) | async-done | bytes 4718608 | tf_op jit(solution)/shard_map/psum | solution.py:9
  234.7 0.0 all-reduce.7.cloned.1.call-update
  234.8 0.0 reduce-scatter.2.cloned.1.call-start
  234.8 248.9 %all-reduce.7.cloned.1.call-done = (f32[768,512]{1,0:T(8,128)}, f32[768,512]{1,0:T(8,128)}, f32[768,512]{1,0:T(8,128)}) async-done(((f32[768,512]{1,0:T(8,128)}, f32[768,512]{1,0:T(8,128)}, f32[768,512]{1,0:T(8,128)}), (f32[768,512]{1,0:T(8,128)}, f32[768,512]{1,0:T(8,128)}, f32[768,512]{1,0:T(8,128)})) %all-reduce.7.cloned.1.call-update) | async-done | bytes 4718608 | tf_op jit(solution)/shard_map/psum | solution.py:9
  483.7 3.2 multiply_convert_fusion.1
  486.9 0.6 fusion.8
  487.5 0.3 copy-done.1
  487.8 1.8 convolution_add_fusion
  489.6 0.0 reduce-scatter.2.cloned.1.call-update
  489.6 0.6 fusion.1
  490.2 1.0 copy.9
  491.3 1.7 fusion.2
  493.0 1.0 copy.10
  494.0 3.3 convolution_convert_fusion
  497.3 212.9 %reduce-scatter.2.cloned.1.call-done = f32[24,512]{1,0:T(8,128)} async-done(((f32[768,512]{1,0:T(8,128)}), f32[24,512]{1,0:T(8,128)}) %reduce-scatter.2.cloned.1.call-update) | async-done | bytes 49168 | tf_op jit(solution)/shard_map/reduce_scatter | solution.py:49
  710.2 1.4 convert_element_type.29
  (7 shorter events, 0.0 us)
Async XLA Ops:
  7.2 104.9 %copy-start = (bf16[512,512]{1,0:T(8,128)(2,1)S(1)}, bf16[512,512]{1,0:T(8,128)(2,1)}, u32[]{:S(2)}) copy-start(bf16[512,512]{1,0:T(8,128)(2,1)} %param.7) | copy-start | bytes 1572868
  7.2 227.6 %all-reduce.5.cloned.1.call-start = ((), (), s32[]{:S(2)}) async-start(), calls=%async_computation.2 | async-start | bytes 9437184 | tf_op jit(solution)/shard_map/psum | solution.py:9
  112.0 1.7 copy-start.2
  113.8 1.8 copy-start.3
  117.3 366.3 %all-reduce.7.cloned.1.call-start = ((), (), s32[]{:S(2)}) async-start(), calls=%async_computation.3 | async-start | bytes 9437184 | tf_op jit(solution)/shard_map/psum | solution.py:9
  234.8 475.4 %reduce-scatter.2.cloned.1.call-start = ((), (), s32[]{:S(2)}) async-start(), calls=%async_computation.1 | async-start | bytes 1622016 | tf_op jit(solution)/shard_map/reduce_scatter | solution.py:49
  486.9 0.9 copy-start.1
Sparse Core Ops, SparseCore 0:
  117.5 117.2 all-reduce.4
  238.0 245.5 all-reduce.6
  489.8 220.3 reduce-scatter.1

commit v2 on v0

--- a/solution.py
+++ b/solution.py
@@ -1,7 +1,24 @@
+import functools
 import jax
 import jax.numpy as jnp
 from jax import lax
 from jax.sharding import PartitionSpec as P
+
+
+def racks_number(t0, net_axis):
+    shares = jax.lax.psum(1, axis_name=net_axis)
+    lanes = []
+    nth = 0
+    while nth < t0.ndim:
+        lanes.append(shares if nth == 0 else 1)
+        nth = nth + 1
+    known = jax.lax.all_to_all(
+        jnp.tile(t0, lanes), concat_axis=0, axis_name=net_axis, split_axis=0, tiled=True
+    )
+    return known
+
+
+raise_keys = functools.partial(racks_number, net_axis="row")
 
 
 def contract_last(left, right):
@@ -29,7 +46,7 @@
 
 def per_device(inputs, out_grad, gate_weight, up_weight, down_weight):
     input_rows, grad_rows = (
-        lax.all_gather(inputs, "row", axis=0, tiled=True),
+        raise_keys(inputs),
         lax.all_gather(out_grad, "row", axis=0, tiled=True),
     )
     gate_part = jnp.dot(input_rows, gate_weight, preferred_element_type=jnp.float32)

time: 480 us -> 455 us (0.948)
  blocking collectives: 105 us -> 62.2 us
  starting transfers between devices: 0.08 us -> 13.2 us
    all_gather x1 -> x0, blocking collectives: 56.1 us -> none  [per_device(): lax.all_gather(inputs, 'row', axis=0, tiled=True)]
    all_gather x1, blocking collectives: 48.7 us -> 62.2 us  [per_device(): lax.all_gather(out_grad, 'row', axis=0, tiled=True)]
    all_to_all x0 -> x1, starting transfers between devices: none -> 13.2 us  [racks_number(): jax.lax.all_to_all(jnp.tile(t0, lanes), concat_axis=0, axis_name=net_axis...]
  transfers between devices with their start and end apart: 2 -> 3, of which waited for: 2 -> 2; matrix products, arithmetic and copies ran while one was open for 2% -> 2% of each run, Pallas kernels for 0% -> 0%
where the time goes in v2:
time: 455 us
  waiting for transfers between devices  343 us (75%)
  blocking collectives  62.2 us (14%)
  between operations  14.1 us (3%)
  matrix products  13.3 us (3%)
  starting transfers between devices  13.2 us (3%)
  other arithmetic  4.65 us (1%)
    reduce_scatter x1, waiting for transfers between devices, per_device(): lax.psum_scatter(contract_last(gate_grad, gate_weight) + contract_last(up...  217 us
    psum x1, waiting for transfers between devices, per_device(): lax.psum((gate_part, up_part, back_part), ('inw', 'outw'))  126 us
    all_gather x1, blocking collectives, per_device(): lax.all_gather(out_grad, 'row', axis=0, tiled=True)  62.2 us
    all_to_all x1, starting transfers between devices, racks_number(): jax.lax.all_to_all(jnp.tile(t0, lanes), concat_axis=0, axis_name=net_axis...  13.2 us
  transfers between devices with their start and end apart: 3, of which 2 were waited for; matrix products, arithmetic and copies ran while one was open for 2% of the time, Pallas kernels for 0%

profile of v2, /device:TPU:8, one launch (start us, length us, event | category | flops | bytes accessed | tf_op | source)
XLA Modules:
  0.0 454.8 jit_solution(8008415760228083637)
XLA Ops:
  7.2 0.0 copy-start
  7.2 1.7 tile.2
  8.9 13.2 %all-to-all-start = ((bf16[32,24,512]{2,1,0:T(8,128)(2,1)}), bf16[32,24,512]{2,1,0:T(8,128)(2,1)S(1)}, u32[]{:S(2)}, u32[]{:S(2)}) async-start(bf16[32,24,512]{2,1,0:T(8,128)(2,1)} %tile.2), calls=%async_computation | async-start | bytes 1572864 | tf_op jit(solution)/shard_map/all_to_all | solution.py:15
  22.1 0.0 all-reduce.3.cloned.1.call-start
  22.2 62.2 %all_gather.3 = bf16[768,512]{1,0:T(8,128)(2,1)S(1)} all-gather(bf16[24,512]{1,0:T(8,128)(2,1)S(1)} %copy-done.4), channel_id=1, replica_groups=mesh['row'=32,'inw'=8,'outw'=2] {'row'}, dimensions={0}, use_global_device_ids=true | all-gather | bytes 811008 | tf_op jit(solution)/shard_map/all_gather | solution.py:50
  84.3 1.8 fusion.5
  86.1 0.0 all-to-all-done
  86.1 1.7 fusion.7
  87.8 1.8 fusion.6
  89.7 0.0 all-reduce.3.cloned.1.call-update
  89.7 0.0 reduce-scatter.2.cloned.1.call-start
  89.7 125.9 %all-reduce.3.cloned.1.call-done = (f32[768,512]{1,0:T(8,128)}, f32[768,512]{1,0:T(8,128)}, f32[768,512]{1,0:T(8,128)}) async-done(((f32[768,512]{1,0:T(8,128)}, f32[768,512]{1,0:T(8,128)}, f32[768,512]{1,0:T(8,128)}), (f32[768,512]{1,0:T(8,128)}, f32[768,512]{1,0:T(8,128)}, f32[768,512]{1,0:T(8,128)})) %all-reduce.3.cloned.1.call-update) | async-done | bytes 4718608 | tf_op jit(solution)/shard_map/psum | solution.py:55
  215.6 3.2 multiply_convert_fusion.1
  218.9 0.6 fusion.8
  219.5 0.3 copy-done.1
  219.8 1.8 convolution_add_fusion
  221.6 0.0 reduce-scatter.2.cloned.1.call-update
  221.6 0.6 fusion.1
  222.2 1.0 copy.9
  223.2 1.7 fusion.2
  224.9 1.0 copy.10
  225.9 3.3 convolution_convert_fusion
  229.2 217.4 %reduce-scatter.2.cloned.1.call-done = f32[24,512]{1,0:T(8,128)} async-done(((f32[768,512]{1,0:T(8,128)}), f32[24,512]{1,0:T(8,128)}) %reduce-scatter.2.cloned.1.call-update) | async-done | bytes 49168 | tf_op jit(solution)/shard_map/reduce_scatter | solution.py:60
  446.6 1.4 convert_element_type.29
  (8 shorter events, 0.0 us)
Async XLA Ops:
  7.2 79.0 %copy-start = (bf16[512,512]{1,0:T(8,128)(2,1)S(1)}, bf16[512,512]{1,0:T(8,128)(2,1)}, u32[]{:S(2)}) copy-start(bf16[512,512]{1,0:T(8,128)(2,1)} %param.7) | copy-start | bytes 1572868
  7.2 15.0 %copy-start.4 = (bf16[24,512]{1,0:T(8,128)(2,1)S(1)}, bf16[24,512]{1,0:T(8,128)(2,1)}, u32[]{:S(2)}) copy-start(bf16[24,512]{1,0:T(8,128)(2,1)} %param.6) | copy-start | bytes 73732
  7.2 77.2 %copy-start.3 = (bf16[512,512]{1,0:T(8,128)(2,1)S(1)}, bf16[512,512]{1,0:T(8,128)(2,1)}, u32[]{:S(2)}) copy-start(bf16[512,512]{1,0:T(8,128)(2,1)} %param.9) | copy-start | bytes 1572868
  8.9 77.2 %all-to-all-start = ((bf16[32,24,512]{2,1,0:T(8,128)(2,1)}), bf16[32,24,512]{2,1,0:T(8,128)(2,1)S(1)}, u32[]{:S(2)}, u32[]{:S(2)}) async-start(bf16[32,24,512]{2,1,0:T(8,128)(2,1)} %tile.2), calls=%async_computation | async-start | bytes 1572864 | tf_op jit(solution)/shard_map/all_to_all | solution.py:15
  22.1 193.5 %all-reduce.3.cloned.1.call-start = ((), (), s32[]{:S(2)}) async-start(), calls=%async_computation.3 | async-start | bytes 9437184 | tf_op jit(solution)/shard_map/psum | solution.py:55
  86.1 1.7 copy-start.2
  89.7 356.9 %reduce-scatter.2.cloned.1.call-start = ((), (), s32[]{:S(2)}) async-start(), calls=%async_computation.2 | async-start | bytes 1622016 | tf_op jit(solution)/shard_map/reduce_scatter | solution.py:60
  218.9 0.9 copy-start.1
Sparse Core Ops, SparseCore 0:
  89.8 125.7 all-reduce.2
  221.7 224.8 reduce-scatter.1
